TPU v7x, 32 devices: a whole 2x2x4 slice. The times are simulated.
32 devices in a mesh: grp: 2 (over x), dev: 16 (over z, y, core).
Axes of the slice: x: 2, y: 2, z: 4, core: 2. Of those that a mesh axis runs over, the one named last changes fastest.
Arguments:
- frames: bfloat16 [80, 64, 1408], P('dev'), may hold values from -100 to 100
- trained: int32 [80], replicated, may hold values from 0 to 3071, as said below
- frame_of: int32 [6144], P('dev'), may hold values from 0 to 3071, as said below
- token_cache: bfloat16 [6144, 1408], P('dev'), may hold values from -100 to 100
- norm_gains: float32 [2, 1408], P('grp'), may hold values from 0.1 to 1.9
- proj_weights: bfloat16 [2, 1408, 4224], P('grp'), may hold values from -4 to 4
- out_weights: bfloat16 [2, 1408, 1408], P('grp'), may hold values from -0.15625 to 0.15625
- patch_cotangent: bfloat16 [80, 64, 1408], P('dev'), may hold values from -0.119628906 to 0.119628906
- time_cotangent: bfloat16 [6144, 1408], P('dev'), may hold values from -6 to 6
Outputs:
- weight_grad: float32 [2, 1408, 1408], P('grp', 'dev')
Inputs may be any that keep to these rules, and one draw needn't show every extreme that they name: `trained`: 80 different frames of the video; among them, for every k, the frames k * 192 and (k + 1) * 192 - 1. `frame_of`: never falls along the tokens; tokens 4 m to 4 m + 3 belong to frames 2 m and 2 m + 1, each frame having 1 to 3 tokens.
All inputs are finite; a program needn't handle non-finite values.
Results may differ from a plain program's by a relative error of at most 0.0078.
Values may be sent and summed in bfloat16 or wider, within the bound.
A program may use at most 192 MiB of HBM per device.

v0:
```python
import jax
import jax.numpy as jnp
from jax import lax
from jax.sharding import PartitionSpec as P

HEADS = 16
HEAD_DIM = 88
SPAN = 128
EPS = 1e-06
HIGH_PRECISION = lax.Precision.HIGHEST


def from_behind(value, axis, steps):
    count = lax.axis_size(axis)
    initial, last = (max(0, -steps), min(count, count - steps))
    return lax.ppermute(value, axis, [(source, source + steps) for source in range(initial, last)])


def with_halo(array, sides, width):
    for axis, dim in sides:
        size, length = (lax.axis_size(axis), array.shape[dim])
        up = [(i, (i + 1) % size) for i in range(size - 1)]
        down = [(j, i) for i, j in up]
        last = lax.slice_in_dim(array, length - width, length, axis=dim)
        initial = lax.slice_in_dim(array, 0, width, axis=dim)
        before = lax.ppermute(last, axis, up)
        after = lax.ppermute(initial, axis, down)
        array = jnp.concatenate([before, array, after], axis=dim)
    return array


def normalize(rows):
    inverse = lax.rsqrt(jnp.mean(rows * rows, axis=-1, keepdims=True) + EPS)
    return (rows * inverse, inverse)


def when_true(flag, compute):

    def skipped():
        return jax.tree.map(jnp.zeros_like, compute())

    return lax.cond(flag, compute, skipped)


def contract_rows(left, right):
    return lax.dot_general(
        left, right, (((0,), (0,)), ((), ())), preferred_element_type=jnp.float32
    )


def contract_exact(left, right):
    return lax.dot_general(left, right, (((0,), (0,)), ((), ())), precision=HIGH_PRECISION)


def contract_cols(left, right):
    return lax.dot_general(
        left, right, (((1,), (1,)), ((), ())), preferred_element_type=jnp.float32
    )


def stack_windows(extended, count):
    return jnp.stack([extended[block * SPAN : (block + 3) * SPAN] for block in range(count)])


def shards(
    frames,
    trained,
    frame_of,
    token_cache,
    norm_gains,
    proj_weights,
    out_weights,
    patch_cotangent,
    time_cotangent,
):
    spatial = lax.axis_index("grp") == 0
    temporal = jnp.logical_not(spatial)
    norm_gain = norm_gains[0]
    in_proj = proj_weights[0]
    out_proj = out_weights[0]
    width = in_proj.shape[0]
    frame_count, patches, _ = frames.shape
    token_count = token_cache.shape[0]
    nblocks = token_count // SPAN
    score_scale = HEAD_DIM ** (-0.5)
    first_token = lax.axis_index("dev") * token_count
    token_total = lax.axis_size("dev") * token_count
    win_pos = (
        first_token
        + (jnp.arange(nblocks, dtype=jnp.int32)[:, None] - 1) * SPAN
        + jnp.arange(3 * SPAN, dtype=jnp.int32)[None, :]
    )
    win_valid = (win_pos >= 0) & (win_pos < token_total)

    def spatial_forward():
        rows = frames.reshape(frame_count * patches, width).astype(jnp.float32)
        scaled_rows, _ = normalize(rows)
        normed = (scaled_rows * norm_gain).astype(jnp.bfloat16)
        packed = jnp.dot(normed, in_proj, preferred_element_type=jnp.float32).astype(jnp.bfloat16)
        packed = packed.reshape(frame_count, patches, 3, HEADS, HEAD_DIM)
        attention_logits = (
            jnp.einsum(
                "fphd,fqhd->fhpq",
                packed[:, :, 0],
                packed[:, :, 1],
                preferred_element_type=jnp.float32,
            )
            * score_scale
        )
        attention_probs = jax.nn.softmax(attention_logits, axis=-1).astype(jnp.bfloat16)
        attended_output = jnp.einsum(
            "fhpq,fqhd->fphd", attention_probs, packed[:, :, 2], preferred_element_type=jnp.float32
        )
        attended_output = attended_output.astype(jnp.bfloat16).reshape(frame_count * patches, width)
        output = rows + jnp.dot(attended_output, out_proj, preferred_element_type=jnp.float32)
        pooled = jnp.mean(output.reshape(frame_count, patches, width), axis=1).astype(jnp.bfloat16)
        return (pooled, attended_output)

    pooled, spatial_mixed = when_true(spatial, spatial_forward)
    handed = from_behind(pooled, "grp", 1)
    arrived = lax.all_gather(handed, "dev", axis=0, tiled=True)

    def temporal_front():
        selector = (frame_of[:, None] == trained[None, :]).astype(jnp.bfloat16)
        inputs = token_cache.astype(jnp.float32) + jnp.dot(
            selector, arrived, preferred_element_type=jnp.float32
        )
        scaled_rows, inverse = normalize(inputs)
        normed = (scaled_rows * norm_gain).astype(jnp.bfloat16)
        packed = jnp.dot(normed, in_proj, preferred_element_type=jnp.float32).astype(jnp.bfloat16)
        return (selector, scaled_rows, inverse, packed[:, :width], packed[:, width:])

    selector, scaled_rows, inverse, queries, key_value = when_true(temporal, temporal_front)
    extended = with_halo(key_value, (("dev", 0),), SPAN)
    key_window = stack_windows(extended, nblocks)
    key_heads = key_window[..., :width].reshape(nblocks, 3 * SPAN, HEADS, HEAD_DIM)
    value_heads = key_window[..., width:].reshape(nblocks, 3 * SPAN, HEADS, HEAD_DIM)
    query_heads = queries.reshape(nblocks, SPAN, HEADS, HEAD_DIM)

    def temporal_attend():
        attention_logits = (
            jnp.einsum(
                "bqhd,bkhd->bhqk", query_heads, key_heads, preferred_element_type=jnp.float32
            )
            * score_scale
        )
        attention_logits = jnp.where(win_valid[:, None, None, :], attention_logits, -1e30)
        row_top = jnp.max(attention_logits, axis=-1, keepdims=True)
        log_total = row_top + jnp.log(
            jnp.sum(jnp.exp(attention_logits - row_top), axis=-1, keepdims=True)
        )
        chances = jnp.exp(attention_logits - log_total)
        chance_weights = chances.astype(jnp.bfloat16)
        attended_output = jnp.einsum(
            "bhqk,bkhd->bqhd", chance_weights, value_heads, preferred_element_type=jnp.float32
        )
        return (
            chances,
            chance_weights,
            log_total[..., 0],
            attended_output.astype(jnp.bfloat16).reshape(token_count, width),
        )

    chances, chance_weights, log_total, time_mixed = when_true(temporal, temporal_attend)

    def temporal_grads():
        grad_mixed = contract_cols(time_cotangent, out_proj).astype(jnp.bfloat16)
        grad_heads = grad_mixed.reshape(nblocks, SPAN, HEADS, HEAD_DIM)
        mixed_heads = time_mixed.reshape(nblocks, SPAN, HEADS, HEAD_DIM)
        row_delta = jnp.sum(
            grad_heads.astype(jnp.float32) * mixed_heads.astype(jnp.float32), axis=-1
        ).transpose(0, 2, 1)
        probability_gradient = jnp.einsum(
            "bqhd,bkhd->bhqk", grad_heads, value_heads, preferred_element_type=jnp.float32
        )
        logit_gradient = (chances * (probability_gradient - row_delta[..., None])).astype(
            jnp.bfloat16
        )
        query_gradient = (
            jnp.einsum(
                "bhqk,bkhd->bqhd", logit_gradient, key_heads, preferred_element_type=jnp.float32
            )
            * score_scale
        )
        return (grad_mixed, row_delta, logit_gradient, query_gradient.reshape(token_count, width))

    grad_mixed, row_delta, logit_gradient, query_gradient = when_true(temporal, temporal_grads)
    stats = jnp.concatenate(
        [
            log_total.transpose(0, 2, 1).reshape(token_count, HEADS),
            row_delta.transpose(0, 2, 1).reshape(token_count, HEADS),
        ],
        axis=-1,
    )
    near_stats = with_halo(stats, (("dev", 0),), SPAN)
    near_rows = with_halo(jnp.concatenate([queries, grad_mixed], axis=-1), (("dev", 0),), SPAN)

    def rim_keys():
        row_window = stack_windows(near_rows, nblocks)
        stat_window = stack_windows(near_stats, nblocks)
        query_part = row_window[..., :width].reshape(nblocks, 3 * SPAN, HEADS, HEAD_DIM)
        grad_part = row_window[..., width:].reshape(nblocks, 3 * SPAN, HEADS, HEAD_DIM)
        totals = stat_window[..., :HEADS].transpose(0, 2, 1)
        deltas = stat_window[..., HEADS:].transpose(0, 2, 1)
        own_keys = key_value[:, :width].reshape(nblocks, SPAN, HEADS, HEAD_DIM)
        own_values = key_value[:, width:].reshape(nblocks, SPAN, HEADS, HEAD_DIM)
        attention_logits = (
            jnp.einsum("bqhd,bkhd->bhqk", query_part, own_keys, preferred_element_type=jnp.float32)
            * score_scale
        )
        again = jnp.where(
            win_valid[:, None, :, None],
            jnp.exp(
                jnp.where(win_valid[:, None, :, None], attention_logits - totals[..., None], 0.0)
            ),
            0.0,
        )
        probability_gradient = jnp.einsum(
            "bqhd,bkhd->bhqk", grad_part, own_values, preferred_element_type=jnp.float32
        )
        part_score = (again * (probability_gradient - deltas[..., None])).astype(jnp.bfloat16)
        key_gradient = (
            jnp.einsum(
                "bhqk,bqhd->bkhd", part_score, query_part, preferred_element_type=jnp.float32
            )
            * score_scale
        )
        value_gradient = jnp.einsum(
            "bhqk,bqhd->bkhd",
            again.astype(jnp.bfloat16),
            grad_part,
            preferred_element_type=jnp.float32,
        )
        return jnp.concatenate(
            [key_gradient.reshape(token_count, width), value_gradient.reshape(token_count, width)],
            axis=-1,
        )

    key_grads = when_true(temporal, rim_keys)

    def temporal_back():
        grad_packed = jnp.concatenate([query_gradient, key_grads], axis=-1).astype(jnp.bfloat16)
        grad_scaled = contract_cols(grad_packed, in_proj) * norm_gain
        grad_inputs = inverse * (
            grad_scaled - scaled_rows * jnp.mean(grad_scaled * scaled_rows, axis=-1, keepdims=True)
        ) + time_cotangent.astype(jnp.float32)
        return contract_exact(selector.astype(jnp.float32), grad_inputs)

    frame_grads = when_true(temporal, temporal_back)
    reduced = lax.psum_scatter(frame_grads, "dev", scatter_dimension=0, tiled=True)
    returned = from_behind(reduced, "grp", -1)

    def spatial_right():
        grads = patch_cotangent.astype(jnp.float32) + returned[:, None, :] / patches
        return grads.reshape(frame_count * patches, width)

    right_side = when_true(spatial, spatial_right)

    def from_frames():
        return contract_exact(spatial_mixed.astype(jnp.float32), right_side)

    def from_tokens():
        return contract_rows(time_mixed, time_cotangent)

    weight_part = lax.psum_scatter(
        lax.cond(spatial, from_frames, from_tokens), "dev", scatter_dimension=0, tiled=True
    )
    return weight_part[None]


def solution(mesh):
    in_specs = (
        P("dev", None, None),
        P(),
        P("dev"),
        P("dev", None),
        P("grp", None),
        P("grp", None, None),
        P("grp", None, None),
        P("dev", None, None),
        P("dev", None),
    )
    out_specs = P("grp", "dev", None)
    return jax.shard_map(shards, mesh=mesh, in_specs=in_specs, out_specs=out_specs, check_vma=False)
```

profile of v0, /device:TPU:0, one launch (start us, length us, event | category | flops | bytes accessed | tf_op | source)
XLA Modules:
  0.0 491.3 jit_solution(10621586428022382250)
XLA Ops:
  6.5 40.0 %conditional.8 = (bf16[5,1408]{1,0:T(8,128)(2,1)S(1)}, bf16[320,1408]{1,0:T(8,128)(2,1)}) conditional(s32[]{:T(128)} %convert_element_type.90, () %tuple.65, (bf16[5,64,1408]{2,1,0:T(8,128)(2,1)}, f32[1,1408]{1,0:T(1,128)}, bf16[1408,4224]{1,0:T(8,128)(2,1)}, bf16[1408,1408]{1,0:T(8,128)(2,1)}) %tuple.143), branch_computations={%region_0.0_spmd, %region_1.0_spmd} | conditional | flops 5198732288 | bytes 54580020 | solution.py:42
  10.3 9.1 %convolution_convert_fusion.1 = bf16[320,4224]{1,0:T(8,128)(2,1)S(1)} fusion(bf16[320,1408]{1,0:T(8,128)(2,1)S(1)} %fusion.44, bf16[1408,4224]{1,0:T(8,128)(2,1)} %get-tuple-element.100), kind=kOutput, calls=%fused_computation.55 | convolution fusion | flops 3807682560 | bytes 15499264 | tf_op jit(solution)/shard_map/cond/branch_1_fun/dot_general | solution.py:99
  19.4 8.5 %reshape.116 = bf16[5,64,3,16,88]{4,3,2,1,0:T(8,128)(2,1)} reshape(bf16[320,4224]{1,0:T(8,128)(2,1)S(1)} %convolution_convert_fusion.1) | data formatting | bytes 5406720 | tf_op jit(solution)/shard_map/cond/branch_1_fun/reshape | solution.py:100
  27.9 3.0 fusion.76
  31.8 3.9 fusion.77
  37.4 2.2 reshape.117
  39.6 5.3 %convolution_add_fusion = f32[320,1408]{1,0:T(8,128)} fusion(bf16[320,1408]{1,0:T(8,128)(2,1)} %reshape.117, bf16[1408,1408]{1,0:T(8,128)(2,1)} %get-tuple-element.101, bf16[320,1408]{1,0:T(8,128)(2,1)S(1)} %bitcast.144), kind=kOutput, calls=%fused_computation.56 | convolution fusion | flops 1269678080 | bytes 7569408 | tf_op jit(solution)/shard_map/cond/branch_1_fun/dot_general | solution.py:115
  44.9 1.6 reduce_sum.58
  49.3 24.1 %all-gather = bf16[16,5,1408]{2,1,0:T(8,128)(2,1)S(1)} all-gather(bf16[1,5,1408]{2,1,0:T(8,128)(2,1)S(1)} %bitcast.152), channel_id=1, replica_groups=mesh['grp'=2,'dev'=16] {'dev'}, dimensions={0}, use_global_device_ids=true | all-gather | bytes 239360 | tf_op jit(solution)/shard_map/all_gather | solution.py:121
  73.5 4.5 conditional.9
  73.6 1.5 broadcast.148
  75.2 1.5 reshape.119
  79.4 2.9 copy.69
  83.3 3.1 collective-permute-start.1
  87.7 2.3 constant_dynamic-update-slice_fusion.1
  90.6 1.8 fusion.70
  94.3 1.7 copy-done
  96.0 6.1 %conditional.10 = (f32[3,16,128,384]{3,2,1,0:T(8,128)}, f32[3,16,128]{2,1,0:T(8,128)S(1)}, bf16[384,1408]{0,1:T(8,128)(2,1)}) conditional(s32[]{:T(128)} %convert_element_type.91, () %tuple.63, (pred[3,384]{1,0:T(4,128)(4,1)S(1)}, bf16[3,128,16,88]{1,0,3,2:T(4,128)(2,1)}, bf16[3,384,16,88]{1,3,2,0:T(8,128)(2,1)S(1)}, ...), branch_computations={%region_9.0_spmd, %region_10.13_spmd} | conditional | flops 856958976 | bytes 60534224 | solution.py:42
  96.0 4.8 broadcast.154
  102.1 6.0 %conditional.11 = (f32[3,16,128]{2,0,1:T(4,128)S(1)}, bf16[384,1408]{0,1:T(8,128)(2,1)}, bf16[384,1408]{0,1:T(8,128)(2,1)}) conditional(s32[]{:T(128)} %convert_element_type.91, () %tuple.72, (bf16[384,1408]{1,0:T(8,128)(2,1)}, bf16[1408,1408]{1,0:T(8,128)(2,1)}, bf16[384,1408]{0,1:T(8,128)(2,1)}, bf16[3,384,16,88]{1,3,2,0:T(8,128)(2,1)}, ...), branch_computations={%region_13.14_spmd, %region_14.16_spmd} | conditional | flops 2363320320 | bytes 39649360 | solution.py:42
  108.0 2.3 constant_dynamic-update-slice_fusion
  110.4 1.6 fusion.79
  111.9 13.2 %collective-permute-start.3 = (bf16[128,2816]{0,1:T(8,128)(2,1)S(1)}, bf16[128,2816]{0,1:T(8,128)(2,1)S(1)}, u32[]{:S(2)}, u32[]{:S(2)}) collective-permute-start(bf16[128,2816]{0,1:T(8,128)(2,1)S(1)} %get-tuple-element.261), channel_id=1, source_target_pairs={{0,1},{1,2},{2,3},{3,4},{4,5},{5,6},{6,7},{7,8},{8,9},{9,10},{10,1... | collective-permute-start | bytes 2162696 | tf_op jit(solution)/shard_map/ppermute | solution.py:26
  126.5 5.0 %collective-permute-start.5 = (f32[128,32]{0,1:T(8,128)S(1)}, f32[128,32]{0,1:T(8,128)S(1)}, u32[]{:S(2)}, u32[]{:S(2)}) collective-permute-start(f32[128,32]{0,1:T(8,128)S(1)} %get-tuple-element.267), channel_id=1, source_target_pairs={{0,1},{1,2},{2,3},{3,4},{4,5},{5,6},{6,7},{7,8},{8,9},{9,10},{10,1... | collective-permute-start | bytes 49160 | tf_op jit(solution)/shard_map/ppermute | solution.py:26
  132.7 3.0 collective-permute-done.6
  135.8 2.1 pad_maximum_fusion.4
  139.0 8.4 %conditional.13 = (f32[80,1408]{1,0:T(8,128)}) conditional(s32[]{:T(128)} %convert_element_type.91, () %tuple.71, (f32[384,1]{0,1:T(1,128)S(1)}, bf16[384,1408]{0,1:T(8,128)(2,1)}, bf16[384,2816]{0,1:T(8,128)(2,1)S(1)}, bf16[1408,4224]{1,0:T(8,128)(2,1)}, f32[1,1408]{1,0:T(1,128)}, /*index=5*/f32[384,1408]{1,0:T(8,128)}, ...), branch_computations={%region_18.19_spmd, %region_19.21_spmd} | conditional | flops 5097455616 | bytes 36246600 | solution.py:42
  148.7 213.6 %all-reduce.4.cloned.1.call-done = f32[80,1408]{1,0:T(8,128)} async-done(((f32[80,1408]{1,0:T(8,128)}), f32[80,1408]{1,0:T(8,128)}) %all-reduce.4.cloned.1.call-update) | async-done | bytes 450576
  364.5 4.7 collective-permute-done.7
  370.6 10.3 %conditional.15 = (f32[1408,1408]{1,0:T(8,128)}) conditional(s32[]{:T(128)} %convert_element_type.90, (bf16[384,1408]{0,1:T(8,128)(2,1)}, bf16[384,1408]{1,0:T(8,128)(2,1)S(1)}) %tuple.137, (bf16[320,1408]{1,0:T(8,128)(2,1)}, f32[320,1408]{1,0:T(8,128)S(1)}) %tuple.78), branch_computations={%region_24.25_spmd, %region_25.26_spmd} | conditional | flops 7612661760 | bytes 10633224 | solution.py:266
  370.6 10.3 %fusion.83 = f32[1408,1408]{1,0:T(8,128)} fusion(bf16[320,1408]{1,0:T(8,128)(2,1)} %get-tuple-element.136, f32[320,1408]{1,0:T(8,128)S(1)} %get-tuple-element.137), kind=kOutput, calls=%fused_computation.129 | convolution fusion | flops 7612661760 | bytes 10633216 | tf_op jit(solution)/shard_map/cond/branch_1_fun/dot_general | solution.py:52
  381.0 103.3 %reduce-scatter.4.cloned.1.call-done = f32[88,1408]{1,0:T(8,128)} async-done(((f32[1408,1408]{1,0:T(8,128)}), f32[88,1408]{1,0:T(8,128)}) %reduce-scatter.4.cloned.1.call-update) | async-done | bytes 495632
  (68 shorter events, 30.1 us)
Async XLA Ops:
  6.5 355.7 %all-reduce.4.cloned.1.call-start = ((), (), s32[]{:S(2)}) async-start(), calls=%async_computation.1 | async-start | bytes 901120
  6.5 67.0 %copy-start.15 = (s32[384]{0:T(512)S(1)}, s32[384]{0:T(512)}, u32[]{:S(2)}) copy-start(s32[384]{0:T(512)} %param.27) | copy-start | bytes 4612
  6.5 67.0 %copy-start.16 = (s32[80]{0:T(128)S(1)}, s32[80]{0:T(128)}, u32[]{:S(2)}) copy-start(s32[80]{0:T(128)} %param.26) | copy-start | bytes 964
  36.5 3.1 copy-start.7
  46.5 2.8 collective-permute-start
  78.0 1.3 copy-start.2
  83.3 6.8 %collective-permute-start.1 = (bf16[128,2816]{0,1:T(8,128)(2,1)}, bf16[128,2816]{0,1:T(8,128)(2,1)}, u32[]{:S(2)}, u32[]{:S(2)}) collective-permute-start(bf16[128,2816]{0,1:T(8,128)(2,1)} %get-tuple-element.265), channel_id=1, source_target_pairs={{0,1},{1,2},{2,3},{3,4},{4,5},{5,6},{6,7},{7,8},{8,9},{9,10},{10,1... | collective-permute-start | bytes 2162696 | tf_op jit(solution)/shard_map/ppermute | solution.py:26
  86.4 4.2 collective-permute-start.2
  94.3 1.7 copy-start
  110.4 25.4 %copy-start.1 = (bf16[384,2816]{0,1:T(8,128)(2,1)S(1)}, bf16[384,2816]{0,1:T(8,128)(2,1)}, u32[]{:S(2)}) copy-start(bf16[384,2816]{0,1:T(8,128)(2,1)} %constant_dynamic-update-slice_fusion) | copy-start | bytes 6488068
  111.9 23.8 %collective-permute-start.3 = (bf16[128,2816]{0,1:T(8,128)(2,1)S(1)}, bf16[128,2816]{0,1:T(8,128)(2,1)S(1)}, u32[]{:S(2)}, u32[]{:S(2)}) collective-permute-start(bf16[128,2816]{0,1:T(8,128)(2,1)S(1)} %get-tuple-element.261), channel_id=1, source_target_pairs={{0,1},{1,2},{2,3},{3,4},{4,5},{5,6},{6,7},{7,8},{8,9},{9,10},{10,1... | collective-permute-start | bytes 2162696 | tf_op jit(solution)/shard_map/ppermute | solution.py:26
  125.1 10.7 %collective-permute-start.4 = (bf16[128,2816]{0,1:T(8,128)(2,1)S(1)}, bf16[128,2816]{0,1:T(8,128)(2,1)S(1)}, u32[]{:S(2)}, u32[]{:S(2)}) collective-permute-start(bf16[128,2816]{0,1:T(8,128)(2,1)S(1)} %get-tuple-element.262), channel_id=1, source_target_pairs={{1,0},{2,1},{3,2},{4,3},{5,4},{6,5},{7,6},{8,7},{9,8},{10,9},{11,1... | collective-permute-start | bytes 2162696 | tf_op jit(solution)/shard_map/ppermute | solution.py:27
  126.5 6.3 %collective-permute-start.5 = (f32[128,32]{0,1:T(8,128)S(1)}, f32[128,32]{0,1:T(8,128)S(1)}, u32[]{:S(2)}, u32[]{:S(2)}) collective-permute-start(f32[128,32]{0,1:T(8,128)S(1)} %get-tuple-element.267), channel_id=1, source_target_pairs={{0,1},{1,2},{2,3},{3,4},{4,5},{5,6},{6,7},{7,8},{8,9},{9,10},{10,1... | collective-permute-start | bytes 49160 | tf_op jit(solution)/shard_map/ppermute | solution.py:26
  131.4 4.3 collective-permute-start.6
  135.8 2.6 copy-start.3
  139.0 8.5 %copy-start.17 = (u32[32]{0:T(128)S(1)}, u32[32]{0:T(128)}, u32[]{:S(2)}) copy-start(u32[32]{0:T(128)} %constant.101) | copy-start | bytes 388
  147.5 336.8 %reduce-scatter.4.cloned.1.call-start = ((), (), s32[]{:S(2)}) async-start(), calls=%async_computation.2 | async-start | bytes 8425472
  363.2 6.0 %collective-permute-start.7 = (f32[5,1408]{1,0:T(8,128)S(1)}, f32[5,1408]{1,0:T(8,128)S(1)}, u32[]{:S(2)}, u32[]{:S(2)}) collective-permute-start(f32[5,1408]{1,0:T(8,128)S(1)} %constant_dynamic-slice_fusion), channel_id=1, source_target_pairs={{16,0},{17,1},{18,2},{19,3},{20,4},{21,5},{22,6},{23,7},{24,8},{25... | collective-permute-start | bytes 84488 | tf_op jit(solution)/shard_map/ppermute | solution.py:16
  369.1 1.5 copy-start.5
Sparse Core Ops, SparseCore 0:
  147.6 214.6 all-reduce.3
  381.1 103.1 reduce-scatter.3
where the time goes:
time: 500 us; the launch traced here: 491 us
  waiting for transfers between devices  327 us (65%)
  local copies, waits for them, and re-layouts  44.1 us (9%)
  starting transfers between devices  27.7 us (6%)
  matrix products  26.3 us (5%)
  blocking collectives  24.1 us (5%)
  other arithmetic  15.8 us (3%)
  between operations  14.4 us (3%)
  loops' own time  12.3 us (2%)
    unnamed x4, waiting for transfers between devices  317 us
    all_gather x1, blocking collectives, shards(): arrived = lax.all_gather(handed, 'dev', axis=0, tiled=True)  24.1 us
    ppermute x3, starting transfers between devices, with_halo(): before = lax.ppermute(last, axis, up)  21.2 us
    another operation x7, loops' own time, when_true(): return lax.cond(flag, compute, skipped)  12.3 us
    another operation x13, local copies, waits for them, and re-layouts  11.9 us
    dot_general x1, matrix products, contract_exact(): lax.dot_general(left, right, (((0,), (0,)), ((), ())), precision=HIGH_PRE...  10.3 us
  transfers between devices with their start and end apart: 10, of which 6 were waited for; matrix products, arithmetic and copies ran while one was open for 1% of the time, Pallas kernels for 0%

commit v1 on v0

--- a/solution.py
+++ b/solution.py
@@ -118,7 +118,18 @@
 
     pooled, spatial_mixed = when_true(spatial, spatial_forward)
     handed = from_behind(pooled, "grp", 1)
-    arrived = lax.all_gather(handed, "dev", axis=0, tiled=True)
+    outer, raw_out, w_next = (jax.lax.axis_size("dev"), jax.lax.axis_index("dev"), handed.shape[0])
+    inter, prior = (handed, 1)
+    while prior < outer:
+        inter = jnp.concatenate(
+            [
+                inter,
+                jax.lax.ppermute(inter, "dev", [(s, (s - prior) % outer) for s in range(outer)]),
+            ],
+            0,
+        )
+        prior = 2 * prior
+    arrived = jnp.roll(inter, raw_out * w_next, 0)
 
     def temporal_front():
         selector = (frame_of[:, None] == trained[None, :]).astype(jnp.bfloat16)

time: 500 us -> 503 us (level)
  blocking collectives: 24.1 us -> 0 us
  waiting for transfers between devices: 327 us -> 344 us
  starting transfers between devices: 27.7 us -> 36 us
    all_gather x1 -> x0, blocking collectives: 24.1 us -> none  [shards(): arrived = lax.all_gather(handed, 'dev', axis=0, tiled=True)]
    ppermute x0 -> x4, waiting for transfers between devices: none -> 16.8 us  [shards(): jax.lax.ppermute(inter, 'dev', [(s, (s - prior) % outer) for s in range(o...]
    ppermute x0 -> x4, starting transfers between devices: none -> 6.63 us  [shards(): jax.lax.ppermute(inter, 'dev', [(s, (s - prior) % outer) for s in range(o...]
  transfers between devices with their start and end apart: 10 -> 14, of which waited for: 6 -> 10; matrix products, arithmetic and copies ran while one was open for 1% -> 1% of each run, Pallas kernels for 0% -> 0%
where the time goes in v1:
time: 503 us; the launch traced here: 494 us
  waiting for transfers between devices  344 us (68%)
  local copies, waits for them, and re-layouts  45.2 us (9%)
  starting transfers between devices  36 us (7%)
  matrix products  26.3 us (5%)
  other arithmetic  15.9 us (3%)
  between operations  14.6 us (3%)
  loops' own time  12.3 us (2%)
    unnamed x4, waiting for transfers between devices  319 us
    ppermute x3, starting transfers between devices, with_halo(): before = lax.ppermute(last, axis, up)  22.9 us
    ppermute x4, waiting for transfers between devices, shards(): jax.lax.ppermute(inter, 'dev', [(s, (s - prior) % outer) for s in range(o...  16.8 us
    another operation x7, loops' own time, when_true(): return lax.cond(flag, compute, skipped)  12.3 us
    another operation x13, local copies, waits for them, and re-layouts  11.9 us
    dot_general x1, matrix products, contract_exact(): lax.dot_general(left, right, (((0,), (0,)), ((), ())), precision=HIGH_PRE...  10.2 us
  transfers between devices with their start and end apart: 14, of which 10 were waited for; matrix products, arithmetic and copies ran while one was open for 1% of the time, Pallas kernels for 0%

profile of v1, /device:TPU:0, one launch (start us, length us, event | category | flops | bytes accessed | tf_op | source)
XLA Modules:
  0.0 494.0 jit_solution(272811089425823720)
XLA Ops:
  6.5 40.0 %conditional.8 = (bf16[5,1408]{1,0:T(8,128)(2,1)S(1)}, bf16[320,1408]{1,0:T(8,128)(2,1)}) conditional(s32[]{:T(128)} %convert_element_type.90, () %tuple.65, (bf16[5,64,1408]{2,1,0:T(8,128)(2,1)}, f32[1,1408]{1,0:T(1,128)}, bf16[1408,4224]{1,0:T(8,128)(2,1)}, bf16[1408,1408]{1,0:T(8,128)(2,1)}) %tuple.146), branch_computations={%region_0.0_spmd, %region_1.0_spmd} | conditional | flops 5198732288 | bytes 54580020 | solution.py:42
  10.3 9.1 %convolution_convert_fusion.1 = bf16[320,4224]{1,0:T(8,128)(2,1)S(1)} fusion(bf16[320,1408]{1,0:T(8,128)(2,1)S(1)} %fusion.44, bf16[1408,4224]{1,0:T(8,128)(2,1)} %get-tuple-element.100), kind=kOutput, calls=%fused_computation.55 | convolution fusion | flops 3807682560 | bytes 15499264 | tf_op jit(solution)/shard_map/cond/branch_1_fun/dot_general | solution.py:99
  19.4 8.5 %reshape.116 = bf16[5,64,3,16,88]{4,3,2,1,0:T(8,128)(2,1)} reshape(bf16[320,4224]{1,0:T(8,128)(2,1)S(1)} %convolution_convert_fusion.1) | data formatting | bytes 5406720 | tf_op jit(solution)/shard_map/cond/branch_1_fun/reshape | solution.py:100
  27.9 3.0 fusion.78
  31.8 3.9 fusion.79
  37.3 2.2 reshape.117
  39.6 5.3 %convolution_add_fusion = f32[320,1408]{1,0:T(8,128)} fusion(bf16[320,1408]{1,0:T(8,128)(2,1)} %reshape.117, bf16[1408,1408]{1,0:T(8,128)(2,1)} %get-tuple-element.101, bf16[320,1408]{1,0:T(8,128)(2,1)S(1)} %bitcast.142), kind=kOutput, calls=%fused_computation.56 | convolution fusion | flops 1269678080 | bytes 7569408 | tf_op jit(solution)/shard_map/cond/branch_1_fun/dot_general | solution.py:115
  44.9 1.6 reduce_sum.58
  49.3 4.9 collective-permute-start.1
  56.9 2.9 collective-permute-done.2
  60.4 3.9 collective-permute-done.3
  64.5 8.5 %collective-permute-done.4 = bf16[40,1408]{1,0:T(8,128)(2,1)S(1)} collective-permute-done((bf16[40,1408]{1,0:T(8,128)(2,1)S(1)}, bf16[40,1408]{1,0:T(8,128)(2,1)S(1)}, u32[]{:S(2)}, u32[]{:S(2)}) %collective-permute-start.4) | collective-permute-done | bytes 112672 | tf_op jit(solution)/shard_map/ppermute | solution.py:127
  74.1 4.5 conditional.9
  80.0 2.9 copy.72
  83.8 2.8 collective-permute-start.5
  88.0 2.3 constant_dynamic-update-slice_fusion.1
  91.6 1.8 fusion.72
  95.4 1.7 copy-done
  97.1 6.1 %conditional.10 = (f32[3,16,128,384]{3,2,1,0:T(8,128)}, f32[3,16,128]{2,1,0:T(8,128)S(1)}, bf16[384,1408]{0,1:T(8,128)(2,1)}) conditional(s32[]{:T(128)} %convert_element_type.91, () %tuple.63, (pred[3,384]{1,0:T(4,128)(4,1)S(1)}, bf16[3,128,16,88]{1,0,3,2:T(4,128)(2,1)}, bf16[3,384,16,88]{1,3,2,0:T(8,128)(2,1)S(1)}, ...), branch_computations={%region_9.10_spmd, %region_10.13_spmd} | conditional | flops 856958976 | bytes 60534224 | solution.py:42
  97.1 4.8 broadcast.154
  103.2 6.0 %conditional.11 = (f32[3,16,128]{2,0,1:T(4,128)S(1)}, bf16[384,1408]{0,1:T(8,128)(2,1)}, bf16[384,1408]{0,1:T(8,128)(2,1)}) conditional(s32[]{:T(128)} %convert_element_type.91, () %tuple.72, (bf16[384,1408]{1,0:T(8,128)(2,1)}, bf16[1408,1408]{1,0:T(8,128)(2,1)}, bf16[384,1408]{0,1:T(8,128)(2,1)}, bf16[3,384,16,88]{1,3,2,0:T(8,128)(2,1)}, ...), branch_computations={%region_13.14_spmd, %region_14.16_spmd} | conditional | flops 2363320320 | bytes 39649360 | solution.py:42
  109.1 2.3 constant_dynamic-update-slice_fusion
  111.5 1.6 fusion.81
  113.1 14.5 %collective-permute-start.7 = (bf16[128,2816]{0,1:T(8,128)(2,1)S(1)}, bf16[128,2816]{0,1:T(8,128)(2,1)S(1)}, u32[]{:S(2)}, u32[]{:S(2)}) collective-permute-start(bf16[128,2816]{0,1:T(8,128)(2,1)S(1)} %get-tuple-element.292), channel_id=1, source_target_pairs={{0,1},{1,2},{2,3},{3,4},{4,5},{5,6},{6,7},{7,8},{8,9},{9,10},{10,1... | collective-permute-start | bytes 2162696 | tf_op jit(solution)/shard_map/ppermute | solution.py:26
  130.2 5.6 %collective-permute-start.9 = (f32[128,32]{0,1:T(8,128)S(1)}, f32[128,32]{0,1:T(8,128)S(1)}, u32[]{:S(2)}, u32[]{:S(2)}) collective-permute-start(f32[128,32]{0,1:T(8,128)S(1)} %get-tuple-element.298), channel_id=1, source_target_pairs={{0,1},{1,2},{2,3},{3,4},{4,5},{5,6},{6,7},{7,8},{8,9},{9,10},{10,1... | collective-permute-start | bytes 49160 | tf_op jit(solution)/shard_map/ppermute | solution.py:26
  136.7 2.1 pad_maximum_fusion.4
  139.9 8.4 %conditional.13 = (f32[80,1408]{1,0:T(8,128)}) conditional(s32[]{:T(128)} %convert_element_type.91, () %tuple.71, (f32[384,1]{0,1:T(1,128)S(1)}, bf16[384,1408]{0,1:T(8,128)(2,1)}, bf16[384,2816]{0,1:T(8,128)(2,1)S(1)}, bf16[1408,4224]{1,0:T(8,128)(2,1)}, f32[1,1408]{1,0:T(1,128)}, /*index=5*/f32[384,1408]{1,0:T(8,128)}, ...), branch_computations={%region_18.19_spmd, %region_19.21_spmd} | conditional | flops 5097455616 | bytes 36246600 | solution.py:42
  149.7 215.4 %all-reduce.4.cloned.1.call-done = f32[80,1408]{1,0:T(8,128)} async-done(((f32[80,1408]{1,0:T(8,128)}), f32[80,1408]{1,0:T(8,128)}) %all-reduce.4.cloned.1.call-update) | async-done | bytes 450576
  367.3 4.7 collective-permute-done.11
  373.5 10.2 %conditional.15 = (f32[1408,1408]{1,0:T(8,128)}) conditional(s32[]{:T(128)} %convert_element_type.90, (bf16[384,1408]{0,1:T(8,128)(2,1)}, bf16[384,1408]{1,0:T(8,128)(2,1)S(1)}) %tuple.140, (bf16[320,1408]{1,0:T(8,128)(2,1)}, f32[320,1408]{1,0:T(8,128)S(1)}) %tuple.78), branch_computations={%region_24.25_spmd, %region_25.26_spmd} | conditional | flops 7612661760 | bytes 10633224 | solution.py:277
  373.5 10.2 %fusion.85 = f32[1408,1408]{1,0:T(8,128)} fusion(bf16[320,1408]{1,0:T(8,128)(2,1)} %get-tuple-element.136, f32[320,1408]{1,0:T(8,128)S(1)} %get-tuple-element.137), kind=kOutput, calls=%fused_computation.134 | convolution fusion | flops 7612661760 | bytes 10633216 | tf_op jit(solution)/shard_map/cond/branch_1_fun/dot_general | solution.py:52
  383.7 103.3 %reduce-scatter.4.cloned.1.call-done = f32[88,1408]{1,0:T(8,128)} async-done(((f32[1408,1408]{1,0:T(8,128)}), f32[88,1408]{1,0:T(8,128)}) %reduce-scatter.4.cloned.1.call-update) | async-done | bytes 495632
  (78 shorter events, 39.2 us)
Async XLA Ops:
  6.5 358.6 %all-reduce.4.cloned.1.call-start = ((), (), s32[]{:S(2)}) async-start(), calls=%async_computation.1 | async-start | bytes 901120
  6.5 67.5 %copy-start.15 = (s32[384]{0:T(512)S(1)}, s32[384]{0:T(512)}, u32[]{:S(2)}) copy-start(s32[384]{0:T(512)} %param.27) | copy-start | bytes 4612
  6.5 67.6 %copy-start.16 = (s32[80]{0:T(128)S(1)}, s32[80]{0:T(128)}, u32[]{:S(2)}) copy-start(s32[80]{0:T(128)} %param.26) | copy-start | bytes 964
  36.5 3.1 copy-start.7
  46.5 2.8 collective-permute-start
  49.3 6.4 %collective-permute-start.1 = (bf16[5,1408]{1,0:T(8,128)(2,1)S(1)}, bf16[5,1408]{1,0:T(8,128)(2,1)S(1)}, u32[]{:S(2)}, u32[]{:S(2)}) collective-permute-start(bf16[5,1408]{1,0:T(8,128)(2,1)S(1)} %collective-permute-done), channel_id=1, source_target_pairs={{0,15},{1,0},{2,1},{3,2},{4,3},{5,4},{6,5},{7,6},{8,7},{9,8},{10,9... | collective-permute-start | bytes 42248 | tf_op jit(solution)/shard_map/ppermute | solution.py:127
  55.7 4.1 collective-permute-start.2
  59.9 4.5 collective-permute-start.3
  64.4 8.6 %collective-permute-start.4 = (bf16[40,1408]{1,0:T(8,128)(2,1)S(1)}, bf16[40,1408]{1,0:T(8,128)(2,1)S(1)}, u32[]{:S(2)}, u32[]{:S(2)}) collective-permute-start(bf16[40,1408]{1,0:T(8,128)(2,1)S(1)} %pad_maximum_fusion.7), channel_id=1, source_target_pairs={{0,8},{1,9},{2,10},{3,11},{4,12},{5,13},{6,14},{7,15},{8,0},{9,1},... | collective-permute-start | bytes 337928 | tf_op jit(solution)/shard_map/ppermute | solution.py:127
  78.6 1.3 copy-start.2
  83.8 6.6 %collective-permute-start.5 = (bf16[128,2816]{0,1:T(8,128)(2,1)}, bf16[128,2816]{0,1:T(8,128)(2,1)}, u32[]{:S(2)}, u32[]{:S(2)}) collective-permute-start(bf16[128,2816]{0,1:T(8,128)(2,1)} %get-tuple-element.296), channel_id=1, source_target_pairs={{0,1},{1,2},{2,3},{3,4},{4,5},{5,6},{6,7},{7,8},{8,9},{9,10},{10,1... | collective-permute-start | bytes 2162696 | tf_op jit(solution)/shard_map/ppermute | solution.py:26
  86.7 5.0 %collective-permute-start.6 = (bf16[128,2816]{0,1:T(8,128)(2,1)S(1)}, bf16[128,2816]{0,1:T(8,128)(2,1)}, u32[]{:S(2)}, u32[]{:S(2)}) collective-permute-start(bf16[128,2816]{0,1:T(8,128)(2,1)S(1)} %get-tuple-element.297), channel_id=1, source_target_pairs={{1,0},{2,1},{3,2},{4,3},{5,4},{6,5},{7,6},{8,7},{9,8},{10,9},{11,1... | collective-permute-start | bytes 2162696 | tf_op jit(solution)/shard_map/ppermute | solution.py:27
  95.4 1.7 copy-start
  111.5 25.2 %copy-start.1 = (bf16[384,2816]{0,1:T(8,128)(2,1)S(1)}, bf16[384,2816]{0,1:T(8,128)(2,1)}, u32[]{:S(2)}) copy-start(bf16[384,2816]{0,1:T(8,128)(2,1)} %constant_dynamic-update-slice_fusion) | copy-start | bytes 6488068
  113.1 23.6 %collective-permute-start.7 = (bf16[128,2816]{0,1:T(8,128)(2,1)S(1)}, bf16[128,2816]{0,1:T(8,128)(2,1)S(1)}, u32[]{:S(2)}, u32[]{:S(2)}) collective-permute-start(bf16[128,2816]{0,1:T(8,128)(2,1)S(1)} %get-tuple-element.292), channel_id=1, source_target_pairs={{0,1},{1,2},{2,3},{3,4},{4,5},{5,6},{6,7},{7,8},{8,9},{9,10},{10,1... | collective-permute-start | bytes 2162696 | tf_op jit(solution)/shard_map/ppermute | solution.py:26
  127.6 9.1 %collective-permute-start.8 = (bf16[128,2816]{0,1:T(8,128)(2,1)S(1)}, bf16[128,2816]{0,1:T(8,128)(2,1)S(1)}, u32[]{:S(2)}, u32[]{:S(2)}) collective-permute-start(bf16[128,2816]{0,1:T(8,128)(2,1)S(1)} %get-tuple-element.293), channel_id=1, source_target_pairs={{1,0},{2,1},{3,2},{4,3},{5,4},{6,5},{7,6},{8,7},{9,8},{10,9},{11,1... | collective-permute-start | bytes 2162696 | tf_op jit(solution)/shard_map/ppermute | solution.py:27
  128.9 6.9 %collective-permute-start.10 = (f32[128,32]{0,1:T(8,128)S(1)}, f32[128,32]{0,1:T(8,128)S(1)}, u32[]{:S(2)}, u32[]{:S(2)}) collective-permute-start(f32[128,32]{0,1:T(8,128)S(1)} %get-tuple-element.299), channel_id=1, source_target_pairs={{1,0},{2,1},{3,2},{4,3},{5,4},{6,5},{7,6},{8,7},{9,8},{10,9},{11,1... | collective-permute-start | bytes 49160 | tf_op jit(solution)/shard_map/ppermute | solution.py:27
  130.2 6.4 %collective-permute-start.9 = (f32[128,32]{0,1:T(8,128)S(1)}, f32[128,32]{0,1:T(8,128)S(1)}, u32[]{:S(2)}, u32[]{:S(2)}) collective-permute-start(f32[128,32]{0,1:T(8,128)S(1)} %get-tuple-element.298), channel_id=1, source_target_pairs={{0,1},{1,2},{2,3},{3,4},{4,5},{5,6},{6,7},{7,8},{8,9},{9,10},{10,1... | collective-permute-start | bytes 49160 | tf_op jit(solution)/shard_map/ppermute | solution.py:26
  136.6 2.6 copy-start.3
  139.9 8.5 %copy-start.17 = (u32[32]{0:T(128)S(1)}, u32[32]{0:T(128)}, u32[]{:S(2)}) copy-start(u32[32]{0:T(128)} %constant.122) | copy-start | bytes 388
  148.3 338.7 %reduce-scatter.4.cloned.1.call-start = ((), (), s32[]{:S(2)}) async-start(), calls=%async_computation.2 | async-start | bytes 8425472
  366.0 6.0 %collective-permute-start.11 = (f32[5,1408]{1,0:T(8,128)S(1)}, f32[5,1408]{1,0:T(8,128)S(1)}, u32[]{:S(2)}, u32[]{:S(2)}) collective-permute-start(f32[5,1408]{1,0:T(8,128)S(1)} %constant_dynamic-slice_fusion), channel_id=1, source_target_pairs={{16,0},{17,1},{18,2},{19,3},{20,4},{21,5},{22,6},{23,7},{24,8},{25... | collective-permute-start | bytes 84488 | tf_op jit(solution)/shard_map/ppermute | solution.py:16
  372.0 1.5 copy-start.5
Sparse Core Ops, SparseCore 0:
  148.5 216.5 all-reduce.3
  383.9 103.1 reduce-scatter.3
